TPU v7x, 256 devices: a whole 4x4x8 slice. The times are simulated.
256 devices in a mesh: corpus: 128 (over y_lo, z, x, core), rep: 2 (over y_hi).
Axes of the slice: x: 4, y: 4 (y_hi: 2, y_lo: 2; y = y_hi * 2 + y_lo), z: 8, core: 2. Of those that a mesh axis runs over, the one named last changes fastest.
Arguments:
- embeddings: bfloat16 [262144, 1024], P(('corpus', 'rep')), may hold values from -6 to 6
- assignments: int32 [262144], P(('corpus', 'rep')), may hold values from 0 to 2047
- old_centroids: bfloat16 [2048, 1024], P('corpus'), may hold values from -6 to 6
- old_counts: int32 [2048], P('corpus'), may hold values from 1 to 32
Outputs:
- residuals: bfloat16 [262144, 1024], P(('corpus', 'rep'))
- new_centroids: bfloat16 [2048, 1024], P('corpus')
All inputs are finite; a program needn't handle non-finite values.
Results may differ from a plain program's by a relative error of at most 0.0043.
Values may be sent and summed in bfloat16 or wider, within the bound.
A program may use at most 64 MiB of HBM per device.

v0:
```python
import jax
import jax.numpy as jnp
from jax import lax
from jax.sharding import PartitionSpec as P


def refresh(sums, old_rows, old_weights):
    merged = old_weights.astype(jnp.float32)[:, None] * old_rows.astype(jnp.float32) + sums
    scale = lax.rsqrt(jnp.mean(merged * merged, axis=1, keepdims=True) + 1e-06)
    return (merged * scale).astype(jnp.bfloat16)


def body(embeddings, assignments, old_centroids, old_counts):
    owned = old_centroids.shape[0]
    half = owned // lax.axis_size("rep")
    offset = lax.axis_index("rep") * half
    labels = lax.iota(jnp.int32, lax.axis_size(("corpus", "rep")) * half)
    onehot = (assignments[:, None] == labels[None, :]).astype(jnp.bfloat16)
    sums = lax.psum_scatter(
        lax.dot_general(
            onehot, embeddings, (((0,), (0,)), ((), ())), preferred_element_type=jnp.float32
        ),
        ("corpus", "rep"),
        scatter_dimension=0,
        tiled=True,
    )
    old_rows = lax.dynamic_slice_in_dim(old_centroids, offset, half, 0)
    old_weights = lax.dynamic_slice_in_dim(old_counts, offset, half, 0)
    halves = refresh(sums, old_rows, old_weights)
    new_centroids = lax.all_gather(halves, "rep", axis=0, tiled=True)
    table = lax.all_gather(new_centroids, "corpus", axis=0, tiled=True)
    looked = jnp.take(table, assignments, axis=0).astype(jnp.float32)
    residuals = (embeddings.astype(jnp.float32) - looked).astype(jnp.bfloat16)
    return (residuals, new_centroids)


def solution(mesh):
    placed = (P(("corpus", "rep"), None), P(("corpus", "rep")), P("corpus", None), P("corpus"))
    return jax.shard_map(
        body,
        mesh=mesh,
        in_specs=placed,
        out_specs=(P(("corpus", "rep"), None), P("corpus", None)),
        check_vma=False,
    )
```

profile of v0, /device:TPU:1, one launch (start us, length us, event | category | flops | bytes accessed | tf_op | source)
XLA Modules:
  0.0 1575.3 jit_solution(12932102317266594770)
XLA Ops:
  7.2 0.0 reduce-scatter.2.cloned.1.call-start
  7.2 8.5 fusion
  15.7 0.0 copy-start.3
  15.7 0.0 copy-start.1
  15.7 0.0 copy-start.2
  15.7 0.0 reduce-scatter.2.cloned.1.call-update
  15.8 0.0 all-gather.2.cloned.1.call-start
  15.8 0.6 copy-done.3
  16.4 0.1 dynamic-slice_convert_fusion
  16.5 1281.0 %reduce-scatter.2.cloned.1.call-done = f32[8,1024]{1,0:T(8,128)} async-done(((f32[2048,1024]{1,0:T(8,128)}), f32[8,1024]{1,0:T(8,128)}) %reduce-scatter.2.cloned.1.call-update) | async-done | bytes 32784 | tf_op jit(solution)/shard_map/reduce_scatter | solution.py:19
  1297.4 0.0 copy-done.1
  1297.4 0.9 multiply_reduce_fusion
  1298.4 0.8 multiply_convert_fusion
  1299.2 4.9 all_gather.6
  1304.1 0.0 all-gather.2.cloned.1.call-update
  1304.1 0.0 copy-done.2
  1304.1 252.4 %all-gather.2.cloned.1.call-done = bf16[2048,1024]{1,0:T(8,128)(2,1)} async-done(((bf16[16,1024]{1,0:T(8,128)(2,1)}), bf16[2048,1024]{1,0:T(8,128)(2,1)}) %all-gather.2.cloned.1.call-update) | async-done | bytes 4194320 | tf_op jit(solution)/shard_map/all_gather | solution.py:31
  1556.6 7.7 gather_fusion
  1564.3 0.0 copy-start
  1564.3 3.6 subtract_convert_fusion
  1567.9 0.0 copy-done
  1567.9 0.6 copy.7
  (3 shorter events, 0.0 us)
Async XLA Ops:
  7.2 1290.3 %reduce-scatter.2.cloned.1.call-start = ((), (), s32[]{:S(2)}) async-start(), calls=%async_computation.1 | async-start | bytes 8421376 | tf_op jit(solution)/shard_map/reduce_scatter | solution.py:19
  15.7 0.7 copy-start.3
  15.7 1281.7 %copy-start.1 = (bf16[16,1024]{1,0:T(8,128)(2,1)S(1)}, bf16[16,1024]{1,0:T(8,128)(2,1)}, u32[]{:S(2)}) copy-start(bf16[16,1024]{1,0:T(8,128)(2,1)} %param.6) | copy-start | bytes 98308
  15.7 1288.4 %copy-start.2 = (s32[1024]{0:T(1024)S(1)}, s32[1024]{0:T(1024)}, u32[]{:S(2)}) copy-start(s32[1024]{0:T(1024)} %param.5) | copy-start | bytes 12292
  15.8 1540.8 %all-gather.2.cloned.1.call-start = ((), (), s32[]{:S(2)}) async-start(), calls=%async_computation.2 | async-start | bytes 4227072 | tf_op jit(solution)/shard_map/all_gather | solution.py:31
  1564.3 3.6 copy-start
Sparse Core Ops, SparseCore 0:
  15.9 1281.4 reduce-scatter.1
  1304.2 252.2 all-gather.1
where the time goes:
time: 1580 us
  waiting for transfers between devices  1530 us (97%)
    reduce_scatter x1, waiting for transfers between devices, body(): lax.psum_scatter(lax.dot_general(onehot, embeddings, (((0,), (0,)), ((),...  1280 us
    all_gather x1, waiting for transfers between devices, body(): table = lax.all_gather(new_centroids, 'corpus', axis=0, tiled=True)  252 us
  transfers between devices with their start and end apart: 2, of which 2 were waited for; matrix products, arithmetic and copies ran while one was open for 0% of the time, Pallas kernels for 0%

commit v1 on v0

v1 whole, which is shorter than its diff:
```python
import jax
import jax.numpy as jnp
from jax import lax
from jax.experimental import pallas as pl
from jax.experimental.pallas import tpu as pltpu
from jax.sharding import PartitionSpec as P

MESH = pl.DeviceIdType.MESH
F32, BF16, I32 = jnp.float32, jnp.bfloat16, jnp.int32

RING, DEPTH, ROWS = 4, 8, 16
QB = DEPTH * ROWS
PB = RING * QB
NSEM = 72


def place():
    c, r = lax.axis_index("corpus"), lax.axis_index("rep")
    core, x, z, ylo = c % 2, (c // 2) % RING, (c // (2 * RING)) % DEPTH, c // (2 * RING * DEPTH)
    return core, x, r * 2 + ylo, z, r


def device(core, x, y, z):
    return (((y % 2) * DEPTH + z) * RING + x) * 2 + core, y // 2


def label_of(i, core, x, y, z):
    p0, q0 = x + core * (y - x), y + core * (x - y)
    p = (p0 + (i >> 9)) & 3
    q = (q0 + ((i >> 7) & 3)) & 3
    zz = (z + ((i >> 4) & 7)) & 7
    xx, yy = p + core * (q - p), q + core * (p - q)
    return (((((yy & 1) * DEPTH + zz) * RING + xx) * 2 + (yy >> 1)) << 4) + (i & 15)


def kernel(
    emb, asg, old, cnt, out, new_out,
    own, sib, oth, asg_sib, oldx, oldx_in,
    send_p, recv_p, part, red,
    send_q, recv_q, red_q, send_z, recv_z,
    ss_out, ss_in, tab, tab_sib, asg_t, hot, hot_sib, acc, acc_sib, res, res_sib,
    send_sems, recv_sems, local_sems,
):
    core, x, y, z, r = place()
    tokens, half = own.shape
    swap = 1 - core
    p0, q0 = x + core * (y - x), y + core * (x - y)

    def pq(p, q):
        p, q = lax.rem(p + RING, RING), lax.rem(q + RING, RING)
        return device(core, p + core * (q - p), q + core * (p - q), z)

    sibling = device(swap, x, y, z)
    right, left = pq(p0 + 1, q0), pq(p0 - 1, q0)
    up, down = pq(p0, q0 + 1), pq(p0, q0 - 1)
    peers = [device(core, x, y, lax.rem(z + k, DEPTH)) for k in range(1, DEPTH)]

    barrier = pltpu.get_barrier_semaphore()
    everyone = [sibling, right, left, up, down] + peers
    for other in everyone:
        pl.semaphore_signal(barrier, inc=1, device_id=other, device_id_type=MESH)

    mine = pl.ds(pl.multiple_of(core * half, 128), half)
    theirs = pl.ds(pl.multiple_of(swap * half, 128), half)
    load_own = pltpu.make_async_copy(emb.at[:, mine], own, local_sems.at[0])
    load_oth = pltpu.make_async_copy(emb.at[:, theirs], oth, local_sems.at[1])
    load_own.start()
    load_oth.start()

    eye = lax.broadcasted_iota(I32, (ROWS, ROWS), 0) == lax.broadcasted_iota(I32, (ROWS, ROWS), 1)
    weight = jnp.sum(jnp.where(eye, cnt[...].astype(F32), 0.0), axis=1, keepdims=True)
    oldx[...] = weight * old[:, theirs].astype(F32)

    pending = []

    def send(src, dst, to):
        n = len(pending)
        copy = pltpu.make_async_remote_copy(
            src_ref=src, dst_ref=dst, send_sem=send_sems.at[n], recv_sem=recv_sems.at[n],
            device_id=to, device_id_type=MESH,
        )
        copy.start()
        pending.append(copy)
        return copy

    pl.semaphore_wait(barrier, len(everyone))
    got_emb = send(emb.at[:, theirs], sib, sibling)
    got_asg = send(asg, asg_sib, sibling)
    got_old = send(oldx, oldx_in, sibling)

    hb = PB // 2
    ready = []

    def chunk(relp, h):
        i = lax.broadcasted_iota(I32, (hb, 1), 0) + (relp * PB + h * hb)
        labels = label_of(i, core, x, y, z)
        if not ready:
            load_own.wait()
        mine_hot = (labels == asg[...]).astype(F32).astype(BF16)
        total = jnp.dot(mine_hot, own[...], preferred_element_type=F32)
        if not ready:
            got_asg.wait_recv()
            got_emb.wait_recv()
            ready.append(True)
        their_hot = (labels == asg_sib[...]).astype(F32).astype(BF16)
        return total + jnp.dot(their_hot, sib[...], preferred_element_type=F32)

    send_p[0] = chunk(2, 0).astype(BF16)
    r1 = send(send_p.at[0], recv_p.at[0], right)
    send_p[1] = chunk(2, 1).astype(BF16)
    l1 = send(send_p.at[1], recv_p.at[1], left)
    send_p[2] = chunk(1, 1).astype(BF16)
    r2 = send(send_p.at[2], recv_p.at[2], right)
    send_p[3] = chunk(3, 0).astype(BF16)
    l2 = send(send_p.at[3], recv_p.at[3], left)
    part[0] = chunk(1, 0)
    part[1] = chunk(3, 1)
    r1.wait_recv()
    send_p[4] = (part[0] + recv_p[0].astype(F32)).astype(BF16)
    r3 = send(send_p.at[4], recv_p.at[4], right)
    l1.wait_recv()
    send_p[5] = (part[1] + recv_p[1].astype(F32)).astype(BF16)
    l3 = send(send_p.at[5], recv_p.at[5], left)
    red[0:hb, :] = chunk(0, 0)
    red[hb:PB, :] = chunk(0, 1)

    for t in range(tokens // 128):
        row = jnp.broadcast_to(asg[:, t * 128 : (t + 1) * 128], (128, 128))
        asg_t[t * 128 : (t + 1) * 128, :] = row.T

    def fill(b, carry):
        i = lax.broadcasted_iota(I32, (1, 128), 1) + b * 128
        lanes = pl.ds(pl.multiple_of(b * 128, 128), 128)
        hot[:, lanes] = (asg_t[...] == label_of(i, core, x, y, z)).astype(F32).astype(BF16)
        hot_sib[:, lanes] = (asg_t[...] == label_of(i, swap, x, y, z)).astype(F32).astype(BF16)
        return carry

    lax.fori_loop(0, RING * PB // 128, fill, 0)

    r2.wait_recv()
    l3.wait_recv()
    red[hb:PB, :] = red[hb:PB, :] + (recv_p[2].astype(F32) + recv_p[5].astype(F32))
    hq = QB // 2

    def piece(relq, h):
        return red[relq * QB + h * hq : relq * QB + (h + 1) * hq, :]

    send_q[0] = piece(2, 0).astype(BF16)
    r1 = send(send_q.at[0], recv_q.at[0], up)
    send_q[1] = piece(2, 1).astype(BF16)
    l1 = send(send_q.at[1], recv_q.at[1], down)
    send_q[3] = piece(3, 0).astype(BF16)
    down2 = send(send_q.at[3], recv_q.at[3], down)
    l2.wait_recv()
    r3.wait_recv()
    red[0:hb, :] = red[0:hb, :] + (recv_p[3].astype(F32) + recv_p[4].astype(F32))
    send_q[2] = piece(1, 1).astype(BF16)
    up2 = send(send_q.at[2], recv_q.at[2], up)
    r1.wait_recv()
    send_q[4] = (piece(1, 0) + recv_q[0].astype(F32)).astype(BF16)
    up3 = send(send_q.at[4], recv_q.at[4], up)
    l1.wait_recv()
    send_q[5] = (piece(3, 1) + recv_q[1].astype(F32)).astype(BF16)
    down3 = send(send_q.at[5], recv_q.at[5], down)
    down2.wait_recv()
    up2.wait_recv()
    up3.wait_recv()
    red_q[0:hq, :] = piece(0, 0) + (recv_q[3].astype(F32) + recv_q[4].astype(F32))
    down3.wait_recv()
    red_q[hq:QB, :] = piece(0, 1) + (recv_q[2].astype(F32) + recv_q[5].astype(F32))

    send_z[...] = red_q[...].astype(BF16)
    zs = [
        send(send_z.at[k * ROWS : (k + 1) * ROWS, :], recv_z.at[k * ROWS : (k + 1) * ROWS, :], peers[k - 1])
        for k in range(1, DEPTH)
    ]
    got_old.wait_recv()
    stale = jnp.where(core == r, weight * old[:, mine].astype(F32), oldx_in[...])
    merged = red_q[0:ROWS, :] + stale
    for k in range(1, DEPTH):
        zs[k - 1].wait_recv()
        merged = merged + recv_z[k * ROWS : (k + 1) * ROWS, :].astype(F32)

    ss_out[...] = jnp.broadcast_to(jnp.sum(merged * merged, axis=1, keepdims=True), (ROWS, 128))
    got_ss = send(ss_out, ss_in, sibling)
    got_ss.wait_recv()
    mean = (ss_out[:, 0:1] + ss_in[:, 0:1]) * (1.0 / (2 * half))
    tab[0:ROWS, :] = (merged * lax.rsqrt(mean + 1e-6)).astype(BF16)

    zs = [
        send(tab.at[0:ROWS, :], tab.at[(DEPTH - k) * ROWS : (DEPTH - k + 1) * ROWS, :], peers[k - 1])
        for k in range(1, DEPTH)
    ]
    for copy in zs:
        copy.wait_recv()

    def rows(relp, relq, h=None):
        start = relp * PB + relq * QB
        if h is None:
            return tab.at[start : start + QB, :]
        return tab.at[start + h * hq : start + (h + 1) * hq, :]

    from_left, from_right = {}, {}

    def first_ring(relq):
        from_left[relq] = send(rows(0, relq), rows(3, relq), right)
        from_right[relq] = send(rows(0, relq), rows(1, relq), left)

    q_up = send(rows(0, 0), rows(0, 3), up)
    q_down = send(rows(0, 0), rows(0, 1), down)
    first_ring(0)
    q_up.wait_recv()
    f_up = send(rows(0, 3, 0), rows(0, 2, 0), up)
    first_ring(3)
    q_down.wait_recv()
    f_down = send(rows(0, 1, 1), rows(0, 2, 1), down)
    first_ring(1)
    f_up.wait_recv()
    f_down.wait_recv()
    first_ring(2)

    def pass_on(start, count):
        return send(tab.at[start : start + count, :], tab_sib.at[start : start + count, :], sibling)

    step = 256

    def look(total, which, table, spans, first):
        def body(t, carry):
            tok = pl.ds(pl.multiple_of(t * step, step), step)
            picked = [
                jnp.dot(which[tok, a : a + n], table[a : a + n, :], preferred_element_type=F32) for a, n in spans
            ]
            value = sum(picked[1:], picked[0])
            total[tok, :] = value if first else total[tok, :] + value
            return carry

        lax.fori_loop(0, tokens // step, body, 0)

    sib0 = pass_on(0, PB)
    look(acc, hot, tab, [(0, PB)], True)

    forwards = []
    from_left[0].wait_recv()
    forwards.append(send(rows(3, 0), rows(2, 0), right))
    from_right[0].wait_recv()
    from_right[3].wait_recv()
    forwards.append(send(rows(1, 3), rows(2, 3), left))
    from_left[3].wait_recv()
    from_left[1].wait_recv()
    forwards.append(send(rows(3, 1), rows(2, 1), right))
    from_right[1].wait_recv()
    from_right[2].wait_recv()
    forwards.append(send(rows(1, 2), rows(2, 2), left))
    sib1 = pass_on(PB, PB)
    from_left[2].wait_recv()
    sib3 = pass_on(3 * PB, PB)
    sib0.wait_recv()
    look(acc_sib, hot_sib, tab_sib, [(0, PB)], True)
    look(acc, hot, tab, [(PB, PB), (3 * PB, PB)], False)
    for copy in forwards:
        copy.wait_recv()
    sib2 = pass_on(2 * PB, PB)
    sib1.wait_recv()
    sib3.wait_recv()
    look(acc_sib, hot_sib, tab_sib, [(PB, PB), (3 * PB, PB)], False)
    load_oth.wait()

    stores = []

    def finish(result, total, which, table, passages, columns, sem):
        for t in range(tokens // step):
            tok = slice(t * step, (t + 1) * step)
            picked = jnp.dot(which[tok, 2 * PB : 3 * PB], table[2 * PB : 3 * PB, :], preferred_element_type=F32)
            result[tok, :] = (passages[tok, :].astype(F32) - (total[tok, :] + picked)).astype(BF16)
            store = pltpu.make_async_copy(result.at[tok, :], out.at[tok, columns], local_sems.at[sem + t])
            store.start()
            stores.append(store)

    finish(res, acc, hot, tab, own, mine, 4)
    sib2.wait_recv()
    finish(res_sib, acc_sib, hot_sib, tab_sib, oth, theirs, 8)

    away = lax.rem(core + r, 2) * 2
    a = pl.multiple_of(away * (QB + core * (PB - QB)), ROWS)
    b = pl.multiple_of(away * (QB + swap * (PB - QB)), ROWS)
    left_half = pltpu.make_async_copy(tab.at[pl.ds(a, ROWS), :], new_out.at[:, mine], local_sems.at[2])
    right_half = pltpu.make_async_copy(tab_sib.at[pl.ds(b, ROWS), :], new_out.at[:, theirs], local_sems.at[3])
    left_half.start()
    right_half.start()
    for copy in pending:
        copy.wait_send()
    for store in stores:
        store.wait()
    left_half.wait()
    right_half.wait()


def body(embeddings, assignments, old_centroids, old_counts):
    tokens, width = embeddings.shape
    half, table = width // 2, RING * PB
    vmem = pltpu.VMEM
    return pl.pallas_call(
        kernel,
        out_shape=(
            jax.ShapeDtypeStruct((tokens, width), BF16),
            jax.ShapeDtypeStruct((ROWS, width), BF16),
        ),
        in_specs=[
            pl.BlockSpec(memory_space=pl.ANY),
            pl.BlockSpec(memory_space=vmem),
            pl.BlockSpec(memory_space=vmem),
            pl.BlockSpec(memory_space=vmem),
        ],
        out_specs=(pl.BlockSpec(memory_space=pl.ANY), pl.BlockSpec(memory_space=pl.ANY)),
        scratch_shapes=[
            vmem((tokens, half), BF16),
            vmem((tokens, half), BF16),
            vmem((tokens, half), BF16),
            vmem((1, tokens), I32),
            vmem((ROWS, half), F32),
            vmem((ROWS, half), F32),
            vmem((6, PB // 2, half), BF16),
            vmem((6, PB // 2, half), BF16),
            vmem((2, PB // 2, half), F32),
            vmem((PB, half), F32),
            vmem((6, QB // 2, half), BF16),
            vmem((6, QB // 2, half), BF16),
            vmem((QB, half), F32),
            vmem((QB, half), BF16),
            vmem((QB, half), BF16),
            vmem((ROWS, 128), F32),
            vmem((ROWS, 128), F32),
            vmem((table, half), BF16),
            vmem((table, half), BF16),
            vmem((tokens, 128), I32),
            vmem((tokens, table), BF16),
            vmem((tokens, table), BF16),
            vmem((tokens, half), F32),
            vmem((tokens, half), F32),
            vmem((tokens, half), BF16),
            vmem((tokens, half), BF16),
            pltpu.SemaphoreType.DMA((NSEM,)),
            pltpu.SemaphoreType.DMA((NSEM,)),
            pltpu.SemaphoreType.DMA((12,)),
        ],
        compiler_params=pltpu.CompilerParams(
            collective_id=0, has_side_effects=True, vmem_limit_bytes=58 * 1024 * 1024
        ),
        cost_estimate=pl.CostEstimate(flops=8 * 2**30, bytes_accessed=4 * 2**20, transcendentals=0),
    )(embeddings, assignments.reshape(1, tokens), old_centroids, old_counts.reshape(1, ROWS))


def solution(mesh):
    placed = (P(("corpus", "rep"), None), P(("corpus", "rep")), P("corpus", None), P("corpus"))
    return jax.shard_map(
        body,
        mesh=mesh,
        in_specs=placed,
        out_specs=(P(("corpus", "rep"), None), P("corpus", None)),
        check_vma=False,
    )
```

time: 1580 us -> 72.5 us (0.05)
  waiting for transfers between devices: 1530 us -> 0 us
  Pallas kernels: 0 us -> 67.9 us
    reduce_scatter x1 -> x0, waiting for transfers between devices: 1280 us -> none  [body(): lax.psum_scatter(lax.dot_general(onehot, embeddings, (((0,), (0,)), ((),...]
    all_gather x1 -> x0, waiting for transfers between devices: 252 us -> none  [body(): table = lax.all_gather(new_centroids, 'corpus', axis=0, tiled=True)]
    pallas_call x0 -> x1, Pallas kernels: none -> 67.9 us  [body(): pl.pallas_call(kernel, out_shape=(jax.ShapeDtypeStruct((tokens, width), B...]
  transfers between devices with their start and end apart: 2 -> 0, of which waited for: 2 -> 0; matrix products, arithmetic and copies ran while one was open for 0% -> 0% of each run, Pallas kernels for 0% -> 0%
where the time goes in v1:
time: 72.5 us; the launch traced here: 72.3 us
  Pallas kernels  67.9 us (94%)
  local copies, waits for them, and re-layouts  3.7 us (5%)
    pallas_call x1, Pallas kernels, body(): pl.pallas_call(kernel, out_shape=(jax.ShapeDtypeStruct((tokens, width), B...  67.9 us
    unnamed x4, local copies, waits for them, and re-layouts  3.7 us

profile of v1, /device:TPU:1, one launch (start us, length us, event | category | flops | bytes accessed | tf_op | source)
XLA Modules:
  0.0 72.3 jit_solution(12169576268525476645)
XLA Ops:
  0.6 67.9 %shard_map.59 = (bf16[1024,1024]{1,0:T(8,128)(2,1)}, bf16[16,1024]{1,0:T(8,128)(2,1)}) custom-call(bf16[1024,1024]{1,0:T(8,128)(2,1)} %emb.1, s32[1,1024]{1,0:T(1,128)} %bitcast.2, bf16[16,1024]{1,0:T(8,128)(2,1)} %old.1, s32[1,16]{1,0:T(1,128)} %bitcast.3), custom_call_target="tpu_custom_call" | custom-call | flops 8589934592 | bytes 4194304 | tf_op jit(solution)/shard_map/pallas_call | solution.py:302
  68.6 0.0 copy-start
  68.6 3.1 %copy.8 = bf16[1024,1024]{1,0:T(8,128)(2,1)} copy(bf16[1024,1024]{1,0:T(8,128)(2,1)} %get-tuple-element.4) | data formatting | bytes 4194304
  71.7 0.0 copy-done
  71.7 0.6 copy.9
Async XLA Ops:
  68.6 3.1 %copy-start = (bf16[16,1024]{1,0:T(8,128)(2,1)S(1)}, bf16[16,1024]{1,0:T(8,128)(2,1)}, u32[]{:S(2)}) copy-start(bf16[16,1024]{1,0:T(8,128)(2,1)} %get-tuple-element.5) | copy-start | bytes 98308

commit v2 on v0

v2 whole, which is shorter than its diff:
```python
import jax
import jax.numpy as jnp
from jax import lax
from jax.experimental import pallas as pl
from jax.experimental.pallas import tpu as pltpu
from jax.sharding import PartitionSpec as P

MESH = pl.DeviceIdType.MESH
F32, BF16, I32, I16 = jnp.float32, jnp.bfloat16, jnp.int32, jnp.int16

RING, DEPTH, ROWS = 4, 8, 16
PIECE = DEPTH // 2 * ROWS
HALF = RING * PIECE
PB = 2 * HALF
HOME = 5
TOP = ROWS // 2


def place():
    c, r = lax.axis_index("corpus"), lax.axis_index("rep")
    core, x, z, ylo = c % 2, (c // 2) % RING, (c // (2 * RING)) % DEPTH, c // (2 * RING * DEPTH)
    return core, x, r * 2 + ylo, z, r


def device(core, x, y, z):
    return (((y % 2) * DEPTH + z) * RING + x) * 2 + core, y // 2


def label_of(i, core, x, y, z):
    p0, q0 = x + core * (y - x), y + core * (x - y)
    p = (p0 + (i >> 9)) & 3
    q = (q0 + 3 - ((i >> 6) & 3)) & 3
    zz = (z + 3 + ((i >> 4) & 3) + ((i >> 6) & 4)) & 7
    xx, yy = p + core * (q - p), q + core * (p - q)
    return (((((yy & 1) * DEPTH + zz) * RING + xx) * 2 + (yy >> 1)) << 4) + (i & 15)


def label_parts(i, core, x, y, z):
    q = ((y + core * (x - y)) + 3 - ((i >> 6) & 3)) & 3
    zz = (z + 3 + ((i >> 4) & 3) + ((i >> 6) & 4)) & 7
    first = ((((q & 1) * DEPTH + zz) * RING * 2 + (q >> 1)) << 4) + (i & 15)
    second = (((zz * RING + q) * 2) << 4) + (i & 15)
    return first + core * (second - first)


def shift_of(p, core):
    first = p * 2 * ROWS
    second = (p % 2) * (DEPTH * RING * 2 * ROWS) + (p // 2) * ROWS
    return first + core * (second - first)


def spot(relp, zh, qs):
    return relp * PB + zh * HALF + qs * PIECE


def kernel(
    emb, asg_in, old_in, cnt_in, out, new_out,
    own, sib, oth, asg, asg_sib, old, cnt, prod, old_sib,
    labels, hot_p, send_p, recv_p, part, send_q, recv_q, send_z, recv_z, send_g, recv_g,
    tab, tab_sib, asg_t, hot, hot_sib,
    load_sems, send_sems, swap_sems, near_sems, far_sems, ring_sems, across_sems, line_sems,
    gather_sems, pass_sems, share_sems,
):
    core, x, y, z, r = place()
    tokens, half = own.shape
    swap = 1 - core
    p0, q0 = x + core * (y - x), y + core * (x - y)

    def pq(p, q):
        p, q = lax.rem(p, RING), lax.rem(q, RING)
        return device(core, p + core * (q - p), q + core * (p - q), z)

    sibling = device(swap, x, y, z)
    right, left = pq(p0 + 1, q0), pq(p0 + 3, q0)
    around = [None] + [pq(p0, q0 + d) for d in range(1, RING)]
    line = {
        (k, c): device(swap if c else core, x, y, lax.rem(z + k, DEPTH))
        for k in range(DEPTH) for c in range(2) if k + c
    }

    barrier = pltpu.get_barrier_semaphore()
    everyone = [right, left] + around[1:] + [line[key] for key in line]
    for other in everyone:
        pl.semaphore_signal(barrier, inc=1, device_id=other, device_id_type=MESH)

    mine = pl.ds(pl.multiple_of(core * half, 128), half)
    theirs = pl.ds(pl.multiple_of(swap * half, 128), half)
    loads = [
        pltpu.make_async_copy(a, b, load_sems.at[n])
        for n, (a, b) in enumerate(
            [(asg_in, asg), (emb.at[:, mine], own), (old_in, old), (cnt_in, cnt), (emb.at[:, theirs], oth)]
        )
    ]
    for load in loads:
        load.start()

    def send(src, dst, to, group, sem):
        copy = pltpu.make_async_remote_copy(
            src_ref=src, dst_ref=dst, send_sem=send_sems.at[group], recv_sem=sem,
            device_id=to, device_id_type=MESH,
        )
        copy.start()
        return copy

    def drain(ref, sem):
        pltpu.make_async_copy(ref, ref, sem).wait()

    pl.semaphore_wait(barrier, len(everyone))
    got_asg = send(asg_in, asg_sib, sibling, 0, swap_sems.at[0])
    got_emb = send(emb.at[:, theirs], sib, sibling, 1, swap_sems.at[1])

    i = lax.broadcasted_iota(I32, (PB, 128), 0)
    labels[...] = label_parts(i, core, x, y, z).astype(I16)
    loads[0].wait()
    loads[1].wait()
    one, zero = jnp.bfloat16(1), jnp.bfloat16(0)

    def chunk(relp, zh, first=False):
        shift = shift_of(lax.rem(p0 + relp, RING), core)
        wanted = labels[zh * HALF : (zh + 1) * HALF, :]

        def hot_rows(ids, base):
            moved = (ids[...] - shift).astype(I16)
            for t in range(0, tokens, 128):
                hot_p[:, base + t : base + t + 128] = jnp.where(wanted == moved[:, t : t + 128], one, zero)

        hot_rows(asg, 0)
        total = jnp.dot(hot_p[:, 0:tokens], own[...], preferred_element_type=F32)
        if first:
            got_asg.wait_recv()
        hot_rows(asg_sib, tokens)
        if first:
            got_emb.wait_recv()
        return total + jnp.dot(hot_p[:, tokens : 2 * tokens], sib[...], preferred_element_type=F32)

    def band(qs):
        return slice(qs * PIECE, (qs + 1) * PIECE)

    def ring(n, to, qs, sem):
        return send(send_p.at[n, band(qs), :], recv_p.at[n, band(qs), :], to, 2, sem)

    send_p[0] = chunk(2, 0, True).astype(BF16)
    r1 = [ring(0, right, qs, near_sems.at[qs]) for qs in range(RING)]
    send_p[1] = chunk(2, 1).astype(BF16)
    l1 = [ring(1, left, qs, near_sems.at[RING + qs]) for qs in range(RING)]
    send_p[2] = chunk(1, 1).astype(BF16)
    for qs in range(RING):
        ring(2, right, qs, far_sems.at[0])
    send_p[3] = chunk(3, 0).astype(BF16)
    for qs in range(RING):
        ring(3, left, qs, far_sems.at[1])
    part[0] = chunk(1, 0)
    part[1] = chunk(3, 1)
    r3, l3 = [], []
    for copies, arrived, n, to in ((r3, r1, 0, right), (l3, l1, 1, left)):
        for qs in range(RING):
            arrived[qs].wait_recv()
            send_p[4 + n, band(qs), :] = (part[n, band(qs), :] + recv_p[n, band(qs), :].astype(F32)).astype(BF16)
            copies.append(ring(4 + n, to, qs, ring_sems.at[n * RING + qs]))
    part[2] = chunk(0, 0)
    part[3] = chunk(0, 1)

    loads[2].wait()
    loads[3].wait()
    eye = lax.broadcasted_iota(I32, (ROWS, ROWS), 0) == lax.broadcasted_iota(I32, (ROWS, ROWS), 1)
    weight = jnp.sum(jnp.where(eye, cnt[...].astype(F32), 0.0), axis=1, keepdims=True)
    prod[...] = weight * old[...].astype(F32)
    my_rows = pl.ds(pl.multiple_of(core * TOP, TOP), TOP)
    their_rows = pl.ds(pl.multiple_of(swap * TOP, TOP), TOP)
    got_old = send(prod.at[their_rows, :], old_sib, sibling, 3, swap_sems.at[2])

    for t in range(0, tokens, 128):
        row = jnp.broadcast_to(asg[:, t : t + 128], (128, 128))
        asg_t[t : t + 128, :] = row.T.astype(I16)

    def fill(low, high):
        def lanes_of(b, carry):
            i = lax.broadcasted_iota(I32, (ROWS, 128), 1) + b * 128
            lanes = pl.ds(pl.multiple_of(b * 128, 128), 128)
            for ref, which in ((hot, core), (hot_sib, swap)):
                row = label_of(i, which, x, y, z).astype(I16)
                ref[:, lanes] = jnp.where(asg_t[...] == row[0:1, :], one, zero)
            return carry

        lax.fori_loop(low, high, lanes_of, 0)

    fill(0, 8)

    drain(recv_p.at[2], far_sems.at[0])
    drain(recv_p.at[3], far_sems.at[1])

    def whole(zh, qs):
        (r3, l3)[zh][qs].wait_recv()
        m, n = (4, 3) if zh == 0 else (5, 2)
        return part[2 + zh, band(qs), :] + (recv_p[m, band(qs), :].astype(F32) + recv_p[n, band(qs), :].astype(F32))

    for zh in range(2):
        for qs in range(RING - 1):
            send_q[zh, band(qs), :] = whole(zh, qs).astype(BF16)
            send(send_q.at[zh, band(qs), :], recv_q.at[zh, band(qs), :], around[3 - qs], 4, across_sems.at[zh])
        part[2 + zh, band(3), :] = whole(zh, 3)

    lower = core == 0

    def fold(v):
        return jnp.concatenate([v[:, : half // 2], v[:, half // 2 :]], axis=0)

    def unfold(v):
        return jnp.concatenate([v[:TOP], v[TOP:]], axis=1)

    home = None
    for zh in range(2):
        value = part[2 + zh, band(3), :]
        drain(recv_q.at[zh, 0 : 3 * PIECE, :], across_sems.at[zh])
        for qs in range(RING - 1):
            value = value + recv_q[zh, band(qs), :].astype(F32)
        for j in range(4):
            k = (zh * 4 + j + 3) % DEPTH
            low, high = value[j * ROWS : j * ROWS + TOP, :], value[j * ROWS + TOP : (j + 1) * ROWS, :]
            for c, v in ((0, jnp.where(lower, low, high)), (1, jnp.where(lower, high, low))):
                if k + c == 0:
                    home = fold(v)
                    continue
                send_z[2 * k + c] = fold(v).astype(BF16)
                send(send_z.at[2 * k + c], recv_z.at[(DEPTH - k) % DEPTH * 2 + c], line[k, c], 5, line_sems.at[0])
    fill(8, 11)
    got_old.wait_recv()
    drain(recv_z.at[1:], line_sems.at[0])
    other = recv_z[1].astype(F32)
    for k in range(1, DEPTH):
        home = home + recv_z[2 * k].astype(F32)
        other = other + recv_z[2 * k + 1].astype(F32)
    held = core == r
    home = unfold(home) + jnp.where(held, prod[my_rows, mine], old_sib[:, mine])
    other = unfold(other) + jnp.where(held, prod[my_rows, theirs], old_sib[:, theirs])
    squares = jnp.sum(home * home, axis=1, keepdims=True) + jnp.sum(other * other, axis=1, keepdims=True)
    scale = lax.rsqrt(squares * (1.0 / (2 * half)) + 1e-6)
    fresh = fold(home * scale).astype(BF16)
    send_g[0] = fresh
    send_g[1] = fold(other * scale).astype(BF16)
    recv_g[0] = fresh

    for k in (4, 3, 5, 2, 6, 1, 7, 0):
        for c in range(2):
            if k + c:
                zh = (HOME - k) % DEPTH // 4
                send(send_g.at[c], recv_g.at[(DEPTH - k) % DEPTH * 2 + c], line[k, c], 6, line_sems.at[1 + zh])
    fill(11, 16)

    def piece(ref, relp, zh, qs):
        start = spot(relp, zh, qs)
        return ref.at[start : start + PIECE, :]

    across, from_left, from_right = {}, {}, {}

    def share(relp, zh, qs):
        send(piece(tab, relp, zh, qs), piece(tab_sib, relp, zh, qs), sibling, 7, share_sems.at[relp])

    def first_ring(zh, qs):
        n = zh * RING + qs
        from_left[zh, qs] = send(piece(tab, 0, zh, qs), piece(tab, 3, zh, qs), right, 8, gather_sems.at[n])
        from_right[zh, qs] = send(piece(tab, 0, zh, qs), piece(tab, 1, zh, qs), left, 8, gather_sems.at[8 + n])
        share(0, zh, qs)

    def pass_on(zh, qs):
        goes_right = (zh + qs) % 2 == 0
        for arrived, relp, to in ((from_left, 3, right), (from_right, 1, left)):
            arrived[zh, qs].wait_recv()
            if (relp == 3) == goes_right:
                send(piece(tab, relp, zh, qs), piece(tab, 2, zh, qs), to, 9, pass_sems.at[zh])
            share(relp, zh, qs)

    for zh in (1, 0):
        drain(recv_g.at[0 : 8 - zh], line_sems.at[1 + zh])
        for j in range(4):
            k = (zh * 4 + j + 3) % DEPTH
            same, sister = unfold(recv_g[2 * k].astype(F32)), unfold(recv_g[2 * k + 1].astype(F32))
            block = jnp.concatenate([jnp.where(lower, same, sister), jnp.where(lower, sister, same)], axis=0)
            start = spot(0, zh, 3) + j * ROWS
            tab[start : start + ROWS, :] = block.astype(BF16)
        for d in (2, 1, 3):
            n = zh * 3 + d - 1
            across[zh, d] = send(
                piece(tab, 0, zh, 3), piece(tab, 0, zh, d - 1), around[d], 10, across_sems.at[2 + n]
            )
        first_ring(zh, 3)
    for zh in (1, 0):
        for d in (1, 3, 2):
            across[zh, d].wait_recv()
            first_ring(zh, d - 1)
        pass_on(zh, 3)

    step = 256

    def look(state, which, table, spans):
        def tile(t, carry):
            tok = pl.ds(pl.multiple_of(t * step, step), step)
            picked = [
                jnp.dot(which[tok, a : a + n], table[a : a + n, :], preferred_element_type=F32) for a, n in spans
            ]
            state[tok, :] = (state[tok, :].astype(F32) - sum(picked[1:], picked[0])).astype(BF16)
            return carry

        lax.fori_loop(0, tokens // step, tile, 0)

    look(own, hot, tab, [(0, PB)])
    loads[4].wait()
    drain(tab.at[0:PB, :], share_sems.at[0])
    look(oth, hot_sib, tab_sib, [(0, PB)])
    for zh in (1, 0):
        for qs in (0, 2, 1):
            pass_on(zh, qs)
    look(own, hot, tab, [(PB, PB), (3 * PB, PB)])
    drain(asg, send_sems.at[0])
    drain(own, send_sems.at[1])
    drain(send_p, send_sems.at[2])
    drain(old_sib, send_sems.at[3])
    drain(send_q.at[:, 0 : 3 * PIECE, :], send_sems.at[4])
    drain(send_z.at[1:], send_sems.at[5])
    drain(send_z.at[1:], send_sems.at[6])
    drain(tab.at[0 : 2 * PB, :], send_sems.at[8])
    drain(tab.at[0 : 6 * PIECE, :], send_sems.at[10])
    drain(tab.at[0:PB, :], share_sems.at[1])
    drain(tab.at[0:PB, :], share_sems.at[3])
    look(oth, hot_sib, tab_sib, [(PB, PB), (3 * PB, PB)])
    last = []
    for zh in (1, 0):
        drain(tab.at[0:HALF, :], pass_sems.at[zh])
        start = spot(2, zh, 0)
        last.append(
            send(tab.at[start : start + HALF, :], tab_sib.at[start : start + HALF, :], sibling, 11 + zh, pass_sems.at[2 + zh])
        )

    def finish(state, which, table, columns):
        def tile(t, carry):
            tok = pl.ds(pl.multiple_of(t * step, step), step)
            picked = jnp.dot(which[tok, 2 * PB : 3 * PB], table[2 * PB : 3 * PB, :], preferred_element_type=F32)
            out[tok, columns] = (state[tok, :].astype(F32) - picked).astype(BF16)
            return carry

        lax.fori_loop(0, tokens // step, tile, 0)

    finish(own, hot, tab, mine)
    for copy in last:
        copy.wait_recv()
    finish(oth, hot_sib, tab_sib, theirs)

    away = lax.rem(core + r, 2) * 2
    base = HALF + (HOME - 4) * ROWS
    a = base + swap * (3 - away) * PIECE + core * (away * PB + 3 * PIECE)
    b = base + core * (3 - away) * PIECE + swap * (away * PB + 3 * PIECE)
    new_out[:, mine] = tab[pl.ds(pl.multiple_of(a, ROWS), ROWS), :]
    new_out[:, theirs] = tab_sib[pl.ds(pl.multiple_of(b, ROWS), ROWS), :]
    drain(tab.at[0 : 3 * PB, :], send_sems.at[7])
    drain(tab.at[0:PB, :], send_sems.at[9])
    for copy in last:
        copy.wait_send()


def body(embeddings, assignments, old_centroids, old_counts):
    tokens, width = embeddings.shape
    half, table = width // 2, RING * PB
    vmem, dma = pltpu.VMEM, pltpu.SemaphoreType.DMA
    operands = (embeddings, assignments.reshape(1, tokens), old_centroids, old_counts.reshape(1, ROWS))
    hbm = pl.BlockSpec(memory_space=pltpu.HBM)
    return pl.pallas_call(
        kernel,
        out_shape=(vmem((tokens, width), BF16), vmem((ROWS, width), BF16)),
        in_specs=[hbm] * 4,
        out_specs=(pl.BlockSpec(memory_space=vmem), pl.BlockSpec(memory_space=vmem)),
        scratch_shapes=[
            vmem((tokens, half), BF16),
            vmem((tokens, half), BF16),
            vmem((tokens, half), BF16),
            vmem((1, tokens), I32),
            vmem((1, tokens), I32),
            vmem((ROWS, width), BF16),
            vmem((1, ROWS), I32),
            vmem((ROWS, width), F32),
            vmem((TOP, width), F32),
            vmem((PB, 128), I16),
            vmem((HALF, 2 * tokens), BF16),
            vmem((6, HALF, half), BF16),
            vmem((6, HALF, half), BF16),
            vmem((4, HALF, half), F32),
            vmem((2, HALF, half), BF16),
            vmem((2, HALF, half), BF16),
            vmem((2 * DEPTH, ROWS, half // 2), BF16),
            vmem((2 * DEPTH, ROWS, half // 2), BF16),
            vmem((2, ROWS, half // 2), BF16),
            vmem((2 * DEPTH, ROWS, half // 2), BF16),
            vmem((table, half), BF16),
            vmem((table, half), BF16),
            vmem((tokens, 128), I16),
            vmem((tokens, table), BF16),
            vmem((tokens, table), BF16),
            dma((5,)),
            dma((13,)),
            dma((3,)),
            dma((8,)),
            dma((2,)),
            dma((8,)),
            dma((8,)),
            dma((3,)),
            dma((16,)),
            dma((4,)),
            dma((4,)),
        ],
        compiler_params=pltpu.CompilerParams(
            collective_id=0, has_side_effects=True, vmem_limit_bytes=58 * 1024 * 1024
        ),
        cost_estimate=pl.CostEstimate(flops=8 * 2**30, bytes_accessed=4 * 2**20, transcendentals=0),
    )(*[pltpu.with_memory_space_constraint(operand, pltpu.HBM) for operand in operands])


def solution(mesh):
    placed = (P(("corpus", "rep"), None), P(("corpus", "rep")), P("corpus", None), P("corpus"))
    return jax.shard_map(
        body,
        mesh=mesh,
        in_specs=placed,
        out_specs=(P(("corpus", "rep"), None), P("corpus", None)),
        check_vma=False,
    )
```

time: 1580 us -> 61.6 us (0.04)
  waiting for transfers between devices: 1530 us -> 0 us
  Pallas kernels: 0 us -> 58.9 us
    reduce_scatter x1 -> x0, waiting for transfers between devices: 1280 us -> none  [body(): lax.psum_scatter(lax.dot_general(onehot, embeddings, (((0,), (0,)), ((),...]
    all_gather x1 -> x0, waiting for transfers between devices: 252 us -> none  [body(): table = lax.all_gather(new_centroids, 'corpus', axis=0, tiled=True)]
    pallas_call x0 -> x1, Pallas kernels: none -> 58.9 us  [body(): pl.pallas_call(kernel, out_shape=(vmem((tokens, width), BF16), vmem((ROWS...]
  transfers between devices with their start and end apart: 2 -> 0, of which waited for: 2 -> 0; matrix products, arithmetic and copies ran while one was open for 0% -> 0% of each run, Pallas kernels for 0% -> 0%
where the time goes in v2:
time: 61.6 us; the launch traced here: 61.5 us
  Pallas kernels  58.9 us (96%)
  local copies, waits for them, and re-layouts  1.94 us (3%)
  between operations  0.64 us (1%)
    pallas_call x1, Pallas kernels, body(): pl.pallas_call(kernel, out_shape=(vmem((tokens, width), BF16), vmem((ROWS...  58.9 us
    unnamed x2, local copies, waits for them, and re-layouts  1.94 us

profile of v2, /device:TPU:1, one launch (start us, length us, event | category | flops | bytes accessed | tf_op | source)
XLA Modules:
  0.0 61.5 jit_solution(15970448483772103051)
XLA Ops:
  0.6 58.9 %shard_map.59 = (bf16[1024,1024]{1,0:T(8,128)(2,1)S(1)}, bf16[16,1024]{1,0:T(8,128)(2,1)S(1)}) custom-call(bf16[1024,1024]{1,0:T(8,128)(2,1)} %emb.1, s32[1,1024]{1,0:T(1,128)} %bitcast.2, bf16[16,1024]{1,0:T(8,128)(2,1)} %old_in.1, s32[1,16]{1,0:T(1,128)} %bitcast.3), custom_call_target="tpu_custom_call" | custom-call | flops 8589934592 | bytes 4194304 | tf_op jit(solution)/shard_map/pallas_call | solution.py:366
  59.6 1.3 %copy.8 = bf16[1024,1024]{1,0:T(8,128)(2,1)} copy(bf16[1024,1024]{1,0:T(8,128)(2,1)S(1)} %get-tuple-element.2) | data formatting | bytes 4194304
  60.9 0.6 copy.9

commit v3 on v2

v3 whole, which is shorter than its diff:
```python
import jax
import jax.numpy as jnp
from jax import lax
from jax.experimental import pallas as pl
from jax.experimental.pallas import tpu as pltpu
from jax.sharding import PartitionSpec as P

MESH = pl.DeviceIdType.MESH
F32, BF16, I32, I16 = jnp.float32, jnp.bfloat16, jnp.int32, jnp.int16

RING, DEPTH, ROWS = 4, 8, 16
PIECE = DEPTH // 2 * ROWS
HALF = RING * PIECE
PB = 2 * HALF
HOME = 5
TOP = ROWS // 2


def place():
    c, r = lax.axis_index("corpus"), lax.axis_index("rep")
    core, x, z, ylo = c % 2, (c // 2) % RING, (c // (2 * RING)) % DEPTH, c // (2 * RING * DEPTH)
    return core, x, r * 2 + ylo, z, r


def device(core, x, y, z):
    return (((y % 2) * DEPTH + z) * RING + x) * 2 + core, y // 2


def label_of(i, turn, x, y, z):
    p0, q0 = x + turn * (y - x), y + turn * (x - y)
    p = (p0 + (i >> 9)) & 3
    q = (q0 + 3 - ((i >> 6) & 3)) & 3
    zz = (z + 3 + ((i >> 4) & 3) + ((i >> 6) & 4)) & 7
    xx, yy = p + turn * (q - p), q + turn * (p - q)
    return (((((yy & 1) * DEPTH + zz) * RING + xx) * 2 + (yy >> 1)) << 4) + (i & 15)


def label_parts(i, turn, x, y, z):
    q = ((y + turn * (x - y)) + 3 - ((i >> 6) & 3)) & 3
    zz = (z + 3 + ((i >> 4) & 3) + ((i >> 6) & 4)) & 7
    first = ((((q & 1) * DEPTH + zz) * RING * 2 + (q >> 1)) << 4) + (i & 15)
    second = (((zz * RING + q) * 2) << 4) + (i & 15)
    return first + turn * (second - first)


def shift_of(p, turn):
    first = p * 2 * ROWS
    second = (p % 2) * (DEPTH * RING * 2 * ROWS) + (p // 2) * ROWS
    return first + turn * (second - first)


def spot(relp, zh, qs):
    return relp * PB + zh * HALF + qs * PIECE


def kernel(
    emb, asg_in, old_in, cnt_in, out, new_out,
    own, sib, oth, asg, asg_sib, old, cnt, prod, old_sib,
    labels, hot_p, send_p, recv_p, part, send_q, recv_q, send_z, recv_z, send_g, recv_g,
    tab, tab_sib, asg_t, hot, hot_sib,
    load_sems, send_sems, swap_sems, near_sems, far_sems, ring_sems, across_sems, line_sems,
    gather_sems, pass_sems, share_sems,
):
    core, x, y, z, r = place()
    tokens, half = own.shape
    quarter = half // 2
    swap = 1 - core
    turns = (core, swap)
    both = range(2)

    def chip(turn, p, q):
        p, q = lax.rem(p, RING), lax.rem(q, RING)
        return device(core, p + turn * (q - p), q + turn * (p - q), z)

    sibling = device(swap, x, y, z)
    first0 = [x + turn * (y - x) for turn in turns]
    second0 = [y + turn * (x - y) for turn in turns]
    right = [chip(turns[g], first0[g] + 1, second0[g]) for g in both]
    left = [chip(turns[g], first0[g] + 3, second0[g]) for g in both]
    around = [[chip(turns[g], first0[g], second0[g] + d) for d in range(RING)] for g in both]
    line = {
        (k, c): device(swap if c else core, x, y, lax.rem(z + k, DEPTH))
        for k in range(DEPTH) for c in range(2) if k + c
    }

    barrier = pltpu.get_barrier_semaphore()
    everyone = around[0][1:] + around[1][1:] + [line[key] for key in line]
    for other in everyone:
        pl.semaphore_signal(barrier, inc=1, device_id=other, device_id_type=MESH)

    def columns_of(side, g):
        return pl.ds(pl.multiple_of(side * half + g * quarter, 128), quarter)

    mine = pl.ds(pl.multiple_of(core * half, 128), half)
    theirs = pl.ds(pl.multiple_of(swap * half, 128), half)
    loads = [
        pltpu.make_async_copy(a, b, load_sems.at[n])
        for n, (a, b) in enumerate(
            [(asg_in, asg), (emb.at[:, mine], own), (old_in, old), (cnt_in, cnt), (emb.at[:, theirs], oth)]
        )
    ]
    for load in loads:
        load.start()

    def send(src, dst, to, group, sem):
        copy = pltpu.make_async_remote_copy(
            src_ref=src, dst_ref=dst, send_sem=send_sems.at[group], recv_sem=sem,
            device_id=to, device_id_type=MESH,
        )
        copy.start()
        return copy

    def drain(ref, sem):
        pltpu.make_async_copy(ref, ref, sem).wait()

    pl.semaphore_wait(barrier, len(everyone))
    got_asg = send(asg_in, asg_sib, sibling, 0, swap_sems.at[0])
    got_emb = send(emb.at[:, theirs], sib, sibling, 1, swap_sems.at[1])

    i = lax.broadcasted_iota(I32, (PB, 128), 0)
    for g in both:
        labels[g] = label_parts(i, turns[g], x, y, z).astype(I16)
    loads[0].wait()
    loads[1].wait()
    one, zero = jnp.bfloat16(1), jnp.bfloat16(0)

    def chunk(g, relp, zh, first=False):
        shift = shift_of(lax.rem(first0[g] + relp, RING), turns[g])
        wanted = labels[g, zh * HALF : (zh + 1) * HALF, :]
        cols = slice(g * quarter, (g + 1) * quarter)

        def hot_rows(ids, base):
            moved = (ids[...] - shift).astype(I16)
            for t in range(0, tokens, 128):
                hot_p[:, base + t : base + t + 128] = jnp.where(wanted == moved[:, t : t + 128], one, zero)

        hot_rows(asg, 0)
        total = jnp.dot(hot_p[:, 0:tokens], own[:, cols], preferred_element_type=F32)
        if first:
            got_asg.wait_recv()
        hot_rows(asg_sib, tokens)
        if first:
            got_emb.wait_recv()
        return total + jnp.dot(hot_p[:, tokens : 2 * tokens], sib[:, cols], preferred_element_type=F32)

    def band(qs):
        return slice(qs * PIECE, (qs + 1) * PIECE)

    def ring(g, n, to, qs, sem):
        return send(send_p.at[g, n, band(qs), :], recv_p.at[g, n, band(qs), :], to[g], 2, sem)

    early = {}
    for n, relp, zh, to in ((0, 2, 0, right), (1, 2, 1, left), (2, 1, 1, right), (3, 3, 0, left)):
        for g in both:
            send_p[g, n] = chunk(g, relp, zh, n + g == 0).astype(BF16)
            for qs in range(RING):
                sem = near_sems.at[(g * 2 + n) * RING + qs] if n < 2 else far_sems.at[g * 2 + n - 2]
                early[g, n, qs] = ring(g, n, to, qs, sem)
    late = {}
    for n, relp, zh, to in ((0, 1, 0, right), (1, 3, 1, left)):
        for g in both:
            part[g, n] = chunk(g, relp, zh)
        for g in both:
            for qs in range(RING):
                early[g, n, qs].wait_recv()
                summed = part[g, n, band(qs), :] + recv_p[g, n, band(qs), :].astype(F32)
                send_p[g, 4 + n, band(qs), :] = summed.astype(BF16)
                late[g, n, qs] = ring(g, 4 + n, to, qs, ring_sems.at[(g * 2 + n) * RING + qs])
    for zh in range(2):
        for g in both:
            part[g, 2 + zh] = chunk(g, 0, zh)

    loads[2].wait()
    loads[3].wait()
    eye = lax.broadcasted_iota(I32, (ROWS, ROWS), 0) == lax.broadcasted_iota(I32, (ROWS, ROWS), 1)
    weight = jnp.sum(jnp.where(eye, cnt[...].astype(F32), 0.0), axis=1, keepdims=True)
    prod[...] = weight * old[...].astype(F32)
    my_rows = pl.ds(pl.multiple_of(core * TOP, TOP), TOP)
    their_rows = pl.ds(pl.multiple_of(swap * TOP, TOP), TOP)
    got_old = send(prod.at[their_rows, :], old_sib, sibling, 3, swap_sems.at[2])

    for t in range(0, tokens, 128):
        row = jnp.broadcast_to(asg[:, t : t + 128], (128, 128))
        asg_t[t : t + 128, :] = row.T.astype(I16)

    def fill(low, high):
        def lanes_of(b, carry):
            i = lax.broadcasted_iota(I32, (ROWS, 128), 1) + b * 128
            lanes = pl.ds(pl.multiple_of(b * 128, 128), 128)
            for ref, which in ((hot, core), (hot_sib, swap)):
                row = label_of(i, which, x, y, z).astype(I16)
                ref[:, lanes] = jnp.where(asg_t[...] == row[0:1, :], one, zero)
            return carry

        lax.fori_loop(low, high, lanes_of, 0)

    fill(0, 6)

    for g in both:
        for n in range(2):
            drain(recv_p.at[g, 2 + n], far_sems.at[g * 2 + n])

    def whole(g, zh, qs):
        late[g, zh, qs].wait_recv()
        m, n = (4, 3) if zh == 0 else (5, 2)
        arrived = recv_p[g, m, band(qs), :].astype(F32) + recv_p[g, n, band(qs), :].astype(F32)
        return part[g, 2 + zh, band(qs), :] + arrived

    for zh in range(2):
        for g in both:
            for qs in range(RING - 1):
                send_q[g, zh, band(qs), :] = whole(g, zh, qs).astype(BF16)
                send(
                    send_q.at[g, zh, band(qs), :], recv_q.at[g, zh, band(qs), :], around[g][3 - qs], 4,
                    across_sems.at[g * 2 + zh],
                )
            part[g, 2 + zh, band(3), :] = whole(g, zh, 3)

    lower = core == 0

    def fold(v):
        return jnp.concatenate([v[0], v[1]], axis=0)

    def unfold(v):
        return [v[:TOP], v[TOP:]]

    home = None
    for zh in range(2):
        value = []
        for g in both:
            v = part[g, 2 + zh, band(3), :]
            drain(recv_q.at[g, zh, 0 : 3 * PIECE, :], across_sems.at[g * 2 + zh])
            for qs in range(RING - 1):
                v = v + recv_q[g, zh, band(qs), :].astype(F32)
            value.append(v)
        for j in range(4):
            k = (zh * 4 + j + 3) % DEPTH
            low = fold([v[j * ROWS : j * ROWS + TOP, :] for v in value])
            high = fold([v[j * ROWS + TOP : (j + 1) * ROWS, :] for v in value])
            for c, v in ((0, jnp.where(lower, low, high)), (1, jnp.where(lower, high, low))):
                if k + c == 0:
                    home = v
                    continue
                send_z[2 * k + c] = v.astype(BF16)
                send(send_z.at[2 * k + c], recv_z.at[(DEPTH - k) % DEPTH * 2 + c], line[k, c], 5, line_sems.at[0])
    fill(6, 10)
    got_old.wait_recv()
    drain(recv_z.at[1:], line_sems.at[0])
    other = recv_z[1].astype(F32)
    for k in range(1, DEPTH):
        home = home + recv_z[2 * k].astype(F32)
        other = other + recv_z[2 * k + 1].astype(F32)
    held = core == r

    def stale(side):
        return fold(
            [jnp.where(held, prod[my_rows, columns_of(side, g)], old_sib[:, columns_of(side, g)]) for g in both]
        )

    home = home + stale(core)
    other = other + stale(swap)
    squares = jnp.sum(home * home + other * other, axis=1, keepdims=True)
    scale = lax.rsqrt((squares[:TOP] + squares[TOP:]) * (1.0 / (2 * half)) + 1e-6)
    scale = fold([scale, scale])
    fresh = (home * scale).astype(BF16)
    send_g[0] = fresh
    send_g[1] = (other * scale).astype(BF16)
    recv_g[0] = fresh

    for k in (4, 3, 5, 2, 6, 1, 7, 0):
        for c in range(2):
            if k + c:
                zh = (HOME - k) % DEPTH // 4
                send(send_g.at[c], recv_g.at[(DEPTH - k) % DEPTH * 2 + c], line[k, c], 6, line_sems.at[1 + zh])
    fill(10, 16)

    def piece(ref, g, relp, zh, qs):
        start = spot(relp, zh, qs)
        return ref.at[g, start : start + PIECE, :]

    across, from_left, from_right = {}, {}, {}

    def share(g, relp, zh, qs):
        send(piece(tab, g, relp, zh, qs), piece(tab_sib, g, relp, zh, qs), sibling, 7, share_sems.at[relp])

    def first_ring(g, zh, qs):
        n = (g * 2 + zh) * RING + qs
        source = piece(tab, g, 0, zh, qs)
        from_left[g, zh, qs] = send(source, piece(tab, g, 3, zh, qs), right[g], 8, gather_sems.at[n])
        from_right[g, zh, qs] = send(source, piece(tab, g, 1, zh, qs), left[g], 8, gather_sems.at[16 + n])

    def pass_on(g, zh, qs):
        goes_right = (zh + qs) % 2 == 0
        for arrived, relp, to in ((from_left, 3, right), (from_right, 1, left)):
            arrived[g, zh, qs].wait_recv()
            if (relp == 3) == goes_right:
                send(piece(tab, g, relp, zh, qs), piece(tab, g, 2, zh, qs), to[g], 9, pass_sems.at[zh])
            share(g, relp, zh, qs)

    for zh in (1, 0):
        drain(recv_g.at[0 : 8 - zh], line_sems.at[1 + zh])
        for j in range(4):
            k = (zh * 4 + j + 3) % DEPTH
            same, sister = unfold(recv_g[2 * k].astype(F32)), unfold(recv_g[2 * k + 1].astype(F32))
            start = spot(0, zh, 3) + j * ROWS
            for g in both:
                upper, under = jnp.where(lower, same[g], sister[g]), jnp.where(lower, sister[g], same[g])
                tab[g, start : start + ROWS, :] = fold([upper, under]).astype(BF16)
        for d in (2, 1, 3):
            for g in both:
                n = (g * 2 + zh) * 3 + d - 1
                across[g, zh, d] = send(
                    piece(tab, g, 0, zh, 3), piece(tab, g, 0, zh, d - 1), around[g][d], 10, across_sems.at[4 + n]
                )
        for g in both:
            first_ring(g, zh, 3)
    for zh in (1, 0):
        for d in (1, 3, 2):
            for g in both:
                across[g, zh, d].wait_recv()
                first_ring(g, zh, d - 1)
        for g in both:
            pass_on(g, zh, 3)
    for zh in (1, 0):
        for qs in (3, 0, 2, 1):
            for g in both:
                share(g, 0, zh, qs)

    step = 256

    def picked(g, whiches, table, tok, relps):
        found = [
            jnp.dot(
                whiches[g][tok, relp * PB : (relp + 1) * PB], table[g, relp * PB : (relp + 1) * PB, :],
                preferred_element_type=F32,
            )
            for relp in relps
        ]
        return sum(found[1:], found[0])

    def look(state, whiches, table, relps):
        def tile(t, carry):
            tok = pl.ds(pl.multiple_of(t * step, step), step)
            for g in both:
                cols = slice(g * quarter, (g + 1) * quarter)
                rest = state[tok, cols].astype(F32) - picked(g, whiches, table, tok, relps)
                state[tok, cols] = rest.astype(BF16)
            return carry

        lax.fori_loop(0, tokens // step, tile, 0)

    hots, hots_sib = (hot, hot_sib), (hot_sib, hot)
    look(own, hots, tab, [0])
    loads[4].wait()
    drain(tab.at[:, 0:PB, :], share_sems.at[0])
    look(oth, hots_sib, tab_sib, [0])
    for zh in (1, 0):
        for qs in (0, 2, 1):
            for g in both:
                pass_on(g, zh, qs)
    look(own, hots, tab, [1, 3])
    drain(asg, send_sems.at[0])
    drain(own, send_sems.at[1])
    drain(send_p, send_sems.at[2])
    drain(old_sib, send_sems.at[3])
    drain(send_q.at[:, :, 0 : 3 * PIECE, :], send_sems.at[4])
    drain(send_z.at[1:], send_sems.at[5])
    drain(send_z.at[1:], send_sems.at[6])
    drain(tab.at[:, 0 : 2 * PB, :], send_sems.at[8])
    drain(tab.at[:, 0 : 6 * PIECE, :], send_sems.at[10])
    drain(tab.at[:, 0:PB, :], share_sems.at[1])
    drain(tab.at[:, 0:PB, :], share_sems.at[3])
    look(oth, hots_sib, tab_sib, [1, 3])
    last = []
    for zh in (1, 0):
        drain(tab.at[:, 0:HALF, :], pass_sems.at[zh])
        there = slice(spot(2, zh, 0), spot(2, zh, 0) + HALF)
        last.append(send(tab.at[:, there, :], tab_sib.at[:, there, :], sibling, 11 + zh, pass_sems.at[2 + zh]))

    def finish(state, whiches, table, side):
        def tile(t, carry):
            tok = pl.ds(pl.multiple_of(t * step, step), step)
            for g in both:
                rest = state[tok, g * quarter : (g + 1) * quarter].astype(F32)
                out[tok, columns_of(side, g)] = (rest - picked(g, whiches, table, tok, [2])).astype(BF16)
            return carry

        lax.fori_loop(0, tokens // step, tile, 0)

    finish(own, hots, tab, core)
    for copy in last:
        copy.wait_recv()
    finish(oth, hots_sib, tab_sib, swap)

    away = lax.rem(core + r, 2) * 2
    base = HALF + (HOME - 4) * ROWS

    def spot_of(turn):
        start = base + (1 - turn) * (3 - away) * PIECE + turn * (away * PB + 3 * PIECE)
        return pl.ds(pl.multiple_of(start, ROWS), ROWS)

    for g in both:
        new_out[:, columns_of(core, g)] = tab[g, spot_of(turns[g]), :]
        new_out[:, columns_of(swap, g)] = tab_sib[g, spot_of(turns[1 - g]), :]
    drain(tab.at[:, 0 : 3 * PB, :], send_sems.at[7])
    drain(tab.at[:, 0:PB, :], send_sems.at[9])
    for copy in last:
        copy.wait_send()


def body(embeddings, assignments, old_centroids, old_counts):
    tokens, width = embeddings.shape
    half, table = width // 2, RING * PB
    vmem, dma = pltpu.VMEM, pltpu.SemaphoreType.DMA
    operands = (embeddings, assignments.reshape(1, tokens), old_centroids, old_counts.reshape(1, ROWS))
    hbm = pl.BlockSpec(memory_space=pltpu.HBM)
    return pl.pallas_call(
        kernel,
        out_shape=(vmem((tokens, width), BF16), vmem((ROWS, width), BF16)),
        in_specs=[hbm] * 4,
        out_specs=(pl.BlockSpec(memory_space=vmem), pl.BlockSpec(memory_space=vmem)),
        scratch_shapes=[
            vmem((tokens, half), BF16),
            vmem((tokens, half), BF16),
            vmem((tokens, half), BF16),
            vmem((1, tokens), I32),
            vmem((1, tokens), I32),
            vmem((ROWS, width), BF16),
            vmem((1, ROWS), I32),
            vmem((ROWS, width), F32),
            vmem((TOP, width), F32),
            vmem((2, PB, 128), I16),
            vmem((HALF, 2 * tokens), BF16),
            vmem((2, 6, HALF, half // 2), BF16),
            vmem((2, 6, HALF, half // 2), BF16),
            vmem((2, 4, HALF, half // 2), F32),
            vmem((2, 2, HALF, half // 2), BF16),
            vmem((2, 2, HALF, half // 2), BF16),
            vmem((2 * DEPTH, ROWS, half // 2), BF16),
            vmem((2 * DEPTH, ROWS, half // 2), BF16),
            vmem((2, ROWS, half // 2), BF16),
            vmem((2 * DEPTH, ROWS, half // 2), BF16),
            vmem((2, table, half // 2), BF16),
            vmem((2, table, half // 2), BF16),
            vmem((tokens, 128), I16),
            vmem((tokens, table), BF16),
            vmem((tokens, table), BF16),
            dma((5,)),
            dma((13,)),
            dma((3,)),
            dma((16,)),
            dma((4,)),
            dma((16,)),
            dma((16,)),
            dma((3,)),
            dma((32,)),
            dma((4,)),
            dma((4,)),
        ],
        compiler_params=pltpu.CompilerParams(
            collective_id=0, has_side_effects=True, vmem_limit_bytes=58 * 1024 * 1024
        ),
        cost_estimate=pl.CostEstimate(flops=8 * 2**30, bytes_accessed=4 * 2**20, transcendentals=0),
    )(*[pltpu.with_memory_space_constraint(operand, pltpu.HBM) for operand in operands])


def solution(mesh):
    placed = (P(("corpus", "rep"), None), P(("corpus", "rep")), P("corpus", None), P("corpus"))
    return jax.shard_map(
        body,
        mesh=mesh,
        in_specs=placed,
        out_specs=(P(("corpus", "rep"), None), P("corpus", None)),
        check_vma=False,
    )
```

time: 61.6 us -> 62.4 us (1.013)
  Pallas kernels: 58.9 us -> 59.7 us
    pallas_call x1, Pallas kernels: 58.9 us -> 59.7 us  [body(): pl.pallas_call(kernel, out_shape=(vmem((tokens, width), BF16), vmem((ROWS...]
where the time goes in v3:
time: 62.4 us; the launch traced here: 62.3 us
  Pallas kernels  59.7 us (96%)
  local copies, waits for them, and re-layouts  1.94 us (3%)
  between operations  0.64 us (1%)
    pallas_call x1, Pallas kernels, body(): pl.pallas_call(kernel, out_shape=(vmem((tokens, width), BF16), vmem((ROWS...  59.7 us
    unnamed x2, local copies, waits for them, and re-layouts  1.94 us

profile of v3, /device:TPU:1, one launch (start us, length us, event | category | flops | bytes accessed | tf_op | source)
XLA Modules:
  0.0 62.3 jit_solution(2217443316673284806)
XLA Ops:
  0.6 59.7 %shard_map.59 = (bf16[1024,1024]{1,0:T(8,128)(2,1)S(1)}, bf16[16,1024]{1,0:T(8,128)(2,1)S(1)}) custom-call(bf16[1024,1024]{1,0:T(8,128)(2,1)} %emb.1, s32[1,1024]{1,0:T(1,128)} %bitcast.2, bf16[16,1024]{1,0:T(8,128)(2,1)} %old_in.1, s32[1,16]{1,0:T(1,128)} %bitcast.3), custom_call_target="tpu_custom_call" | custom-call | flops 8589934592 | bytes 4194304 | tf_op jit(solution)/shard_map/pallas_call | solution.py:417
  60.3 1.3 %copy.8 = bf16[1024,1024]{1,0:T(8,128)(2,1)} copy(bf16[1024,1024]{1,0:T(8,128)(2,1)S(1)} %get-tuple-element.2) | data formatting | bytes 4194304
  61.7 0.6 copy.9

commit v4 on v2

--- a/solution.py
+++ b/solution.py
@@ -107,7 +107,11 @@
 
     pl.semaphore_wait(barrier, len(everyone))
     got_asg = send(asg_in, asg_sib, sibling, 0, swap_sems.at[0])
-    got_emb = send(emb.at[:, theirs], sib, sibling, 1, swap_sems.at[1])
+    tk = tokens // 2
+    got_emb = [
+        send(emb.at[n * tk : (n + 1) * tk, theirs], sib.at[n * tk : (n + 1) * tk, :], sibling, 1, swap_sems.at[1 + 2 * n])
+        for n in range(2)
+    ]
 
     i = lax.broadcasted_iota(I32, (PB, 128), 0)
     labels[...] = label_parts(i, core, x, y, z).astype(I16)
@@ -130,7 +134,11 @@
             got_asg.wait_recv()
         hot_rows(asg_sib, tokens)
         if first:
-            got_emb.wait_recv()
+            for n in range(2):
+                got_emb[n].wait_recv()
+                there = hot_p[:, tokens + n * tk : tokens + (n + 1) * tk]
+                total = total + jnp.dot(there, sib[n * tk : (n + 1) * tk, :], preferred_element_type=F32)
+            return total
         return total + jnp.dot(hot_p[:, tokens : 2 * tokens], sib[...], preferred_element_type=F32)
 
     def band(qs):
@@ -290,7 +298,7 @@
             first_ring(zh, d - 1)
         pass_on(zh, 3)
 
-    step = 256
+    step = 512
 
     def look(state, which, table, spans):
         def tile(t, carry):
@@ -307,10 +315,26 @@
     loads[4].wait()
     drain(tab.at[0:PB, :], share_sems.at[0])
     look(oth, hot_sib, tab_sib, [(0, PB)])
-    for zh in (1, 0):
-        for qs in (0, 2, 1):
-            pass_on(zh, qs)
-    look(own, hot, tab, [(PB, PB), (3 * PB, PB)])
+    for qs in (0, 2, 1):
+        pass_on(1, qs)
+    look(own, hot, tab, [(PB + HALF, HALF), (3 * PB + HALF, HALF)])
+    for qs in (0, 2, 1):
+        pass_on(0, qs)
+    look(own, hot, tab, [(PB, HALF), (3 * PB, HALF)])
+    last = []
+
+    def hand_over(zh):
+        drain(tab.at[0:HALF, :], pass_sems.at[zh])
+        start = spot(2, zh, 0)
+        last.append(
+            send(tab.at[start : start + HALF, :], tab_sib.at[start : start + HALF, :], sibling, 11 + zh, pass_sems.at[2 + zh])
+        )
+
+    drain(tab.at[0:PB, :], share_sems.at[1])
+    drain(tab.at[0:PB, :], share_sems.at[3])
+    hand_over(1)
+    look(oth, hot_sib, tab_sib, [(PB, PB), (3 * PB, PB)])
+    hand_over(0)
     drain(asg, send_sems.at[0])
     drain(own, send_sems.at[1])
     drain(send_p, send_sems.at[2])
@@ -320,16 +344,6 @@
     drain(send_z.at[1:], send_sems.at[6])
     drain(tab.at[0 : 2 * PB, :], send_sems.at[8])
     drain(tab.at[0 : 6 * PIECE, :], send_sems.at[10])
-    drain(tab.at[0:PB, :], share_sems.at[1])
-    drain(tab.at[0:PB, :], share_sems.at[3])
-    look(oth, hot_sib, tab_sib, [(PB, PB), (3 * PB, PB)])
-    last = []
-    for zh in (1, 0):
-        drain(tab.at[0:HALF, :], pass_sems.at[zh])
-        start = spot(2, zh, 0)
-        last.append(
-            send(tab.at[start : start + HALF, :], tab_sib.at[start : start + HALF, :], sibling, 11 + zh, pass_sems.at[2 + zh])
-        )
 
     def finish(state, which, table, columns):
         def tile(t, carry):
@@ -396,7 +410,7 @@
             vmem((tokens, table), BF16),
             dma((5,)),
             dma((13,)),
-            dma((3,)),
+            dma((4,)),
             dma((8,)),
             dma((2,)),
             dma((8,)),

time: 61.6 us -> 59.4 us (0.964)
  Pallas kernels: 58.9 us -> 56.7 us
    pallas_call x1, Pallas kernels: 58.9 us -> 56.7 us  [body(): pl.pallas_call(kernel, out_shape=(vmem((tokens, width), BF16), vmem((ROWS...]
where the time goes in v4:
time: 59.4 us; the launch traced here: 59.3 us
  Pallas kernels  56.7 us (95%)
  local copies, waits for them, and re-layouts  1.94 us (3%)
  between operations  0.64 us (1%)
    pallas_call x1, Pallas kernels, body(): pl.pallas_call(kernel, out_shape=(vmem((tokens, width), BF16), vmem((ROWS...  56.7 us
    unnamed x2, local copies, waits for them, and re-layouts  1.94 us

profile of v4, /device:TPU:1, one launch (start us, length us, event | category | flops | bytes accessed | tf_op | source)
XLA Modules:
  0.0 59.3 jit_solution(15278336554023347480)
XLA Ops:
  0.6 56.7 %shard_map.59 = (bf16[1024,1024]{1,0:T(8,128)(2,1)S(1)}, bf16[16,1024]{1,0:T(8,128)(2,1)S(1)}) custom-call(bf16[1024,1024]{1,0:T(8,128)(2,1)} %emb.1, s32[1,1024]{1,0:T(1,128)} %bitcast.2, bf16[16,1024]{1,0:T(8,128)(2,1)} %old_in.1, s32[1,16]{1,0:T(1,128)} %bitcast.3), custom_call_target="tpu_custom_call" | custom-call | flops 8589934592 | bytes 4194304 | tf_op jit(solution)/shard_map/pallas_call | solution.py:380
  57.3 1.3 %copy.8 = bf16[1024,1024]{1,0:T(8,128)(2,1)} copy(bf16[1024,1024]{1,0:T(8,128)(2,1)S(1)} %get-tuple-element.2) | data formatting | bytes 4194304
  58.7 0.6 %copy.9 = bf16[16,1024]{1,0:T(8,128)(2,1)} copy(bf16[16,1024]{1,0:T(8,128)(2,1)S(1)} %get-tuple-element.3) | data formatting | bytes 65536

commit v5 on v4

--- a/solution.py
+++ b/solution.py
@@ -248,7 +248,7 @@
     send_g[1] = fold(other * scale).astype(BF16)
     recv_g[0] = fresh
 
-    for k in (4, 3, 5, 2, 6, 1, 7, 0):
+    for k in (1, 7, 6, 0, 4, 3, 5, 2):
         for c in range(2):
             if k + c:
                 zh = (HOME - k) % DEPTH // 4

time: 59.4 us -> 58.4 us (0.983)
  Pallas kernels: 56.7 us -> 55.7 us
    pallas_call x1, Pallas kernels: 56.7 us -> 55.7 us  [body(): pl.pallas_call(kernel, out_shape=(vmem((tokens, width), BF16), vmem((ROWS...]
where the time goes in v5:
time: 58.4 us; the launch traced here: 58.3 us
  Pallas kernels  55.7 us (95%)
  local copies, waits for them, and re-layouts  1.94 us (3%)
  between operations  0.64 us (1%)
    pallas_call x1, Pallas kernels, body(): pl.pallas_call(kernel, out_shape=(vmem((tokens, width), BF16), vmem((ROWS...  55.7 us
    unnamed x2, local copies, waits for them, and re-layouts  1.94 us

profile of v5, /device:TPU:1, one launch (start us, length us, event | category | flops | bytes accessed | tf_op | source)
XLA Modules:
  0.0 58.3 jit_solution(17971209475193336002)
XLA Ops:
  0.6 55.7 %shard_map.59 = (bf16[1024,1024]{1,0:T(8,128)(2,1)S(1)}, bf16[16,1024]{1,0:T(8,128)(2,1)S(1)}) custom-call(bf16[1024,1024]{1,0:T(8,128)(2,1)} %emb.1, s32[1,1024]{1,0:T(1,128)} %bitcast.2, bf16[16,1024]{1,0:T(8,128)(2,1)} %old_in.1, s32[1,16]{1,0:T(1,128)} %bitcast.3), custom_call_target="tpu_custom_call" | custom-call | flops 8589934592 | bytes 4194304 | tf_op jit(solution)/shard_map/pallas_call | solution.py:380
  56.3 1.3 %copy.8 = bf16[1024,1024]{1,0:T(8,128)(2,1)} copy(bf16[1024,1024]{1,0:T(8,128)(2,1)S(1)} %get-tuple-element.2) | data formatting | bytes 4194304
  57.7 0.6 %copy.9 = bf16[16,1024]{1,0:T(8,128)(2,1)} copy(bf16[16,1024]{1,0:T(8,128)(2,1)S(1)} %get-tuple-element.3) | data formatting | bytes 65536
